TPU v7x, 32 devices: a whole 2x2x4 slice. The times are simulated.
32 devices in a mesh: img: 4 (over y, core), tile: 8 (over z, x).
Axes of the slice: x: 2, y: 2, z: 4, core: 2. Of those that a mesh axis runs over, the one named last changes fastest.
Arguments:
- tiles: bfloat16 [8192, 1152], P(('img', 'tile')), may hold values from -6 to 6
- tile_image: int32 [32], P(('img', 'tile')), may hold values from 0 to 1
- guide: bfloat16 [8, 512, 1152], P('img', 'tile'), may hold values from -160 to 160
- gain: float32 [1152], replicated, may hold values from 0.5 to 1.5
- w_query: bfloat16 [1152, 1152], replicated, may hold values from -0.1875 to 0.1875
- w_key: bfloat16 [1152, 1152], replicated, may hold values from -0.1875 to 0.1875
- w_value: bfloat16 [1152, 1152], replicated, may hold values from -0.1875 to 0.1875
- w_out: bfloat16 [1152, 1152], replicated, may hold values from -0.1875 to 0.1875
- grad_out: bfloat16 [8192, 1152], P(('img', 'tile')), may hold values from -6 to 6
Outputs:
- grad_tiles: bfloat16 [8192, 1152], P(('img', 'tile'))
- grad_guide: bfloat16 [8, 512, 1152], P('img', 'tile')
- grad_weights: float32 [4, 1152, 1152], P(None, ('img', 'tile'))
- grad_gain: float32 [1152], replicated
Inputs may be any that keep to these rules, and one draw needn't show every extreme that they name: `tile_image`: image of each tile within its own img group of 2 images.
All inputs are finite; a program needn't handle non-finite values.
Results may differ from a plain program's by a relative error of at most 0.034.
The roundings to bfloat16 on the way count: a program that leaves them out, or rounds other values in their place, can miss the bound.
Values may be sent and summed in bfloat16 or wider, within the bound.
A program may use at most 128 MiB of HBM per device.

v0:
```python
import jax
import jax.numpy as jnp
from jax import lax
from jax.sharding import PartitionSpec as P

HEADS = 16
TILE = 256


def tile_pass(q_tile, k_img, v_img, d_tile):
    width = q_tile.shape[1]
    head_size = width // HEADS
    scale = head_size ** (-0.5)
    rows = q_tile.shape[0]
    keyrows = k_img.shape[0]
    qh = q_tile.reshape(rows, HEADS, head_size)
    kh = k_img.reshape(keyrows, HEADS, head_size)
    vh = v_img.reshape(keyrows, HEADS, head_size)
    dh = d_tile.reshape(rows, HEADS, head_size)
    scores = jnp.einsum("qhd,khd->hqk", qh, kh, preferred_element_type=jnp.float32) * scale
    top = jnp.max(scores, axis=-1, keepdims=True)
    expo = jnp.exp(scores - top)
    probs = expo / jnp.sum(expo, axis=-1, keepdims=True)
    pb = probs.astype(jnp.bfloat16)
    outv = jnp.einsum("hqk,khd->qhd", pb, vh, preferred_element_type=jnp.float32).astype(
        jnp.bfloat16
    )
    dprob = jnp.einsum("qhd,khd->hqk", dh, vh, preferred_element_type=jnp.float32)
    delta = jnp.sum(probs * dprob, axis=-1, keepdims=True)
    dscore = (probs * (dprob - delta) * scale).astype(jnp.bfloat16)
    dq = jnp.einsum("hqk,khd->qhd", dscore, kh, preferred_element_type=jnp.float32).astype(
        jnp.bfloat16
    )
    dk = jnp.einsum("hqk,qhd->khd", dscore, qh, preferred_element_type=jnp.float32).reshape(
        keyrows, width
    )
    dv = jnp.einsum("hqk,qhd->khd", pb, dh, preferred_element_type=jnp.float32).reshape(
        keyrows, width
    )
    return (outv.reshape(rows, width), dq.reshape(rows, width), dk, dv)


def project(rows_in, weight):
    flat = rows_in.reshape(-1, rows_in.shape[-1])
    result = jnp.dot(flat, weight, preferred_element_type=jnp.float32).astype(jnp.bfloat16)
    return result.reshape(rows_in.shape)


def on_device(tiles, tile_image, guide, gain, w_query, w_key, w_value, w_out, grad_out):
    width = tiles.shape[1]
    tile_count = tile_image.shape[0]
    xf = tiles.astype(jnp.float32)
    rstd = lax.rsqrt(jnp.mean(xf * xf, axis=-1, keepdims=True) + 1e-06)
    normed = xf * rstd
    hidden = (normed * gain).astype(jnp.bfloat16)
    query = jnp.dot(hidden, w_query, preferred_element_type=jnp.float32).astype(jnp.bfloat16)
    key_part = project(guide, w_key)
    value_part = project(guide, w_value)
    keys, values = (
        lax.all_gather(key_part, "tile", axis=1, tiled=True),
        lax.all_gather(value_part, "tile", axis=1, tiled=True),
    )
    dout = jnp.einsum("td,ed->te", grad_out, w_out, preferred_element_type=jnp.float32).astype(
        jnp.bfloat16
    )

    def step(carry, item):
        dk_acc, dv_acc = carry
        q_tile, d_tile, image = item
        k_img = lax.dynamic_index_in_dim(keys, image, 0, keepdims=False)
        v_img = lax.dynamic_index_in_dim(values, image, 0, keepdims=False)
        outv, dq, dk, dv = tile_pass(q_tile, k_img, v_img, d_tile)
        old_k = lax.dynamic_index_in_dim(dk_acc, image, 0, keepdims=False)
        old_v = lax.dynamic_index_in_dim(dv_acc, image, 0, keepdims=False)
        dk_acc = lax.dynamic_update_index_in_dim(dk_acc, old_k + dk, image, 0)
        dv_acc = lax.dynamic_update_index_in_dim(dv_acc, old_v + dv, image, 0)
        return ((dk_acc, dv_acc), (outv, dq))

    start = (jnp.zeros(keys.shape, jnp.float32), jnp.zeros(keys.shape, jnp.float32))
    items = (
        query.reshape(tile_count, TILE, width),
        dout.reshape(tile_count, TILE, width),
        tile_image,
    )
    (dk_all, dv_all), (outs, dqs) = lax.scan(step, start, items)
    outv = outs.reshape(-1, width)
    dq = dqs.reshape(-1, width)
    dk_mine, dv_mine = (
        lax.psum_scatter(
            dk_all.astype(jnp.bfloat16), "tile", scatter_dimension=1, tiled=True
        ).astype(jnp.float32),
        lax.psum_scatter(
            dv_all.astype(jnp.bfloat16), "tile", scatter_dimension=1, tiled=True
        ).astype(jnp.float32),
    )
    dkb = dk_mine.astype(jnp.bfloat16).reshape(-1, width)
    dvb = dv_mine.astype(jnp.bfloat16).reshape(-1, width)
    flat = guide.reshape(-1, width)
    grad_guide = (
        (
            jnp.einsum("ge,de->gd", dkb, w_key, preferred_element_type=jnp.float32)
            + jnp.einsum("ge,de->gd", dvb, w_value, preferred_element_type=jnp.float32)
        )
        .astype(jnp.bfloat16)
        .reshape(guide.shape)
    )
    dh = jnp.einsum("te,de->td", dq, w_query, preferred_element_type=jnp.float32)
    grad_gain = lax.psum(jnp.sum(dh * normed, axis=0), ("img", "tile"))
    dn = dh * gain
    grad_tiles = (rstd * (dn - normed * jnp.mean(dn * normed, axis=-1, keepdims=True))).astype(
        jnp.bfloat16
    )
    stacked = jnp.stack(
        [
            jnp.einsum("td,te->de", hidden, dq, preferred_element_type=jnp.float32),
            jnp.einsum("td,te->de", flat, dkb, preferred_element_type=jnp.float32),
            jnp.einsum("td,te->de", flat, dvb, preferred_element_type=jnp.float32),
            jnp.einsum("td,te->de", outv, grad_out, preferred_element_type=jnp.float32),
        ]
    )
    partial_sum = lax.psum_scatter(
        stacked.astype(jnp.bfloat16), "img", scatter_dimension=1, tiled=True
    )
    grad_weights = lax.psum_scatter(partial_sum, "tile", scatter_dimension=1, tiled=True).astype(
        jnp.float32
    )
    return (grad_tiles, grad_guide, grad_weights, grad_gain)


def solution(mesh):
    return jax.shard_map(
        on_device,
        mesh=mesh,
        in_specs=(
            P(("img", "tile"), None),
            P(("img", "tile")),
            P("img", "tile", None),
            P(),
            P(),
            P(),
            P(),
            P(),
            P(("img", "tile"), None),
        ),
        out_specs=(
            P(("img", "tile"), None),
            P("img", "tile", None),
            P(None, ("img", "tile"), None),
            P(),
        ),
        check_vma=False,
    )
```

profile of v0, /device:TPU:0, one launch (start us, length us, event | category | flops | bytes accessed | tf_op | source)
XLA Modules:
  0.0 541.6 jit_solution(14714770374273404809)
XLA Ops:
  7.2 3.3 convolution_convert_fusion.5
  10.6 3.1 convolution_convert_fusion.4
  18.7 3.8 convolution_convert_fusion.2
  24.6 40.8 %all-gather.3.cloned.1.call-done = bf16[2,512,1152]{2,1,0:T(8,128)(2,1)} async-done(((bf16[2,64,1152]{2,1,0:T(8,128)(2,1)}), bf16[2,512,1152]{2,1,0:T(8,128)(2,1)}) %all-gather.3.cloned.1.call-update) | async-done | bytes 2359312 | tf_op jit(solution)/shard_map/all_gather | solution.py:60
  70.3 47.9 %all-gather.5.cloned.1.call-done = bf16[2,512,1152]{2,1,0:T(8,128)(2,1)} async-done(((bf16[2,64,1152]{2,1,0:T(8,128)(2,1)}), bf16[2,512,1152]{2,1,0:T(8,128)(2,1)}) %all-gather.5.cloned.1.call-update) | async-done | bytes 2359312 | tf_op jit(solution)/shard_map/all_gather | solution.py:61
  122.9 8.0 %fusion.52 = (f32[16,256]{1,0:T(8,128)}, f32[16,256,512]{2,1,0:T(8,128)}) fusion(bf16[256,16,72]{0,2,1:T(8,128)(2,1)} %bitcast.95, bf16[512,16,72]{0,2,1:T(8,128)(2,1)} %bitcast.90), kind=kOutput, calls=%fused_computation.61 | convolution fusion | flops 308281856 | bytes 10174464 | tf_op jit(solution)/shard_map/while/body/eval_jaxpr/sub | solution.py:22
  130.9 6.0 %fusion.53 = f32[16,256,512]{2,1,0:T(8,128)} fusion(bf16[256,16,72]{0,2,1:T(8,128)(2,1)} %bitcast.85, bf16[512,16,72]{0,2,1:T(8,128)(2,1)} %bitcast.83), kind=kOutput, calls=%fused_computation.62 | convolution fusion | flops 301989888 | bytes 10158080 | tf_op jit(solution)/shard_map/while/body/eval_jaxpr/qhd,khd->hqk/dot_general | solution.py:28
  137.0 34.5 %fusion.16 = bf16[16,72,512]{2,1,0:T(8,128)(2,1)} fusion(bf16[256,16,72]{0,2,1:T(8,128)(2,1)} %bitcast.96, f32[16,256,512]{2,1,0:T(8,128)} %fusion.53, f32[16,256,512]{2,1,0:T(8,128)} %get-tuple-element.45, f32[16,256]{1,0:T(8,128)} %get-tuple-element.44), kind=kOutput, calls=%fused_computation.21 | convolution fusion | flops 316674560 | bytes 18563072 | tf_op jit(solution)/shard_map/while/body/eval_jaxpr/hqk,qhd->khd/dot_general | solution.py:34
  176.9 5.4 fusion.24
  187.5 5.2 fusion.30
  192.7 2.5 fusion.9
  195.2 30.0 %fusion.33 = bf16[16,72,256]{2,1,0:T(8,128)(2,1)} fusion(bf16[512,16,72]{0,2,1:T(8,128)(2,1)} %bitcast.91, f32[16,256,512]{2,1,0:T(8,128)} %fusion.53, f32[16,256,512]{2,1,0:T(8,128)} %get-tuple-element.45, f32[16,256]{1,0:T(8,128)} %get-tuple-element.44), kind=kOutput, calls=%fused_computation.40 | convolution fusion | flops 316969472 | bytes 18563072 | tf_op jit(solution)/shard_map/while/body/eval_jaxpr/hqk,khd->qhd/dot_general | solution.py:31
  225.2 3.7 fusion.8
  228.9 15.5 %reduce-scatter.4.cloned.1.call-done = bf16[2,64,1152]{2,1,0:T(8,128)(2,1)} async-done(((bf16[2,512,1152]{2,1,0:T(8,128)(2,1)}), bf16[2,64,1152]{2,1,0:T(8,128)(2,1)}) %reduce-scatter.4.cloned.1.call-update) | async-done | bytes 294928 | tf_op jit(solution)/shard_map/reduce_scatter | solution.py:89
  244.4 3.3 fusion.7
  247.7 68.1 %reduce-scatter.6.cloned.1.call-done = bf16[2,64,1152]{2,1,0:T(8,128)(2,1)} async-done(((bf16[2,512,1152]{2,1,0:T(8,128)(2,1)}), bf16[2,64,1152]{2,1,0:T(8,128)(2,1)}) %reduce-scatter.6.cloned.1.call-update) | async-done | bytes 294928 | tf_op jit(solution)/shard_map/reduce_scatter | solution.py:92
  317.9 7.6 %pad_maximum_fusion = bf16[4,1152,1152]{2,1,0:T(8,128)(2,1)} fusion(bf16[1,1152,1152]{2,1,0:T(8,128)(2,1)} %fusion.9, bf16[1,1152,1152]{2,1,0:T(8,128)(2,1)S(1)} %fusion.6, bf16[1,1152,1152]{2,1,0:T(8,128)(2,1)S(1)} %copy-done.2, bf16[1,1152,1152]{2,1,0:T(8,128)(2,1)} %fusion.8), kind=kLoop, calls=%fused_computation.2 | loop fusion | flops 15925248 | bytes 21233664 | tf_op jit(solution)/shard_map/stack | solution.py:113
  325.8 85.1 %reduce-scatter.8.cloned.1.call-done = bf16[4,288,1152]{2,1,0:T(8,128)(2,1)} async-done(((bf16[4,1152,1152]{2,1,0:T(8,128)(2,1)}), bf16[4,288,1152]{2,1,0:T(8,128)(2,1)}) %reduce-scatter.8.cloned.1.call-update) | async-done | bytes 2654224 | tf_op jit(solution)/shard_map/reduce_scatter | solution.py:121
  410.9 4.6 copy.41
  417.4 3.9 fusion.41
  421.3 41.9 %psum.7 = f32[1152]{0:T(1024)} all-reduce(f32[1152]{0:T(1024)} %get-tuple-element.42), channel_id=1, replica_groups=mesh['img'=4,'tile'=8] {'img','tile'}, use_global_device_ids=true, to_apply=%region_10.11 | all-reduce | flops 1152 | bytes 9216 | tf_op jit(solution)/shard_map/psum | solution.py:108
  463.3 2.5 fusion.40
  465.8 2.7 fusion.54
  470.1 62.7 %all-reduce.3.cloned.1.call-done = bf16[4,288,1152]{2,0,1:T(4,128)(2,1)} async-done(((bf16[4,288,1152]{2,0,1:T(4,128)(2,1)}), bf16[4,288,1152]{2,0,1:T(4,128)(2,1)}) %all-reduce.3.cloned.1.call-update) | async-done | bytes 2654224
  (56 shorter events, 33.8 us)
Async XLA Ops:
  7.2 7.5 %copy-start = (bf16[1152,1152]{1,0:T(8,128)(2,1)S(1)}, bf16[1152,1152]{1,0:T(8,128)(2,1)}, u32[]{:S(2)}) copy-start(bf16[1152,1152]{1,0:T(8,128)(2,1)} %param.13) | copy-start | bytes 7962628
  7.2 3.5 copy-start.4
  7.2 58.3 %all-gather.3.cloned.1.call-start = ((), (), s32[]{:S(2)}) async-start(), calls=%async_computation.3 | async-start | bytes 2654208 | tf_op jit(solution)/shard_map/all_gather | solution.py:60
  10.6 3.9 copy-start.3
  10.6 4.1 copy-start.9
  10.6 107.6 %all-gather.5.cloned.1.call-start = ((), (), s32[]{:S(2)}) async-start(), calls=%async_computation.4 | async-start | bytes 2654208 | tf_op jit(solution)/shard_map/all_gather | solution.py:61
  13.8 230.6 %reduce-scatter.4.cloned.1.call-start = ((), (), s32[]{:S(2)}) async-start(), calls=%async_computation.5 | async-start | bytes 2654208 | tf_op jit(solution)/shard_map/reduce_scatter | solution.py:89
  173.8 1.7 copy-start.6
  176.6 139.2 %reduce-scatter.6.cloned.1.call-start = ((), (), s32[]{:S(2)}) async-start(), calls=%async_computation.6 | async-start | bytes 2654208 | tf_op jit(solution)/shard_map/reduce_scatter | solution.py:92
  184.6 1.7 copy-start.5
  187.4 223.5 %reduce-scatter.8.cloned.1.call-start = ((), (), s32[]{:S(2)}) async-start(), calls=%async_computation.7 | async-start | bytes 13271040 | tf_op jit(solution)/shard_map/reduce_scatter | solution.py:121
  187.5 5.3 copy-start.10
  315.9 2.0 copy-start.2
  325.5 207.4 %all-reduce.3.cloned.1.call-start = ((), (), s32[]{:S(2)}) async-start(), calls=%async_computation.8 | async-start | bytes 5308416
  415.5 0.7 copy-start.11
  417.4 48.4 %copy-start.7 = (bf16[2,64,1152]{2,1,0:T(8,128)(2,1)S(1)}, bf16[2,64,1152]{2,1,0:T(8,128)(2,1)}, u32[]{:S(2)}) copy-start(bf16[2,64,1152]{2,1,0:T(8,128)(2,1)} %reduce-scatter.4.cloned.1.call-done) | copy-start | bytes 884740
  463.2 5.2 copy-start.1
  463.2 5.2 copy-start.8
Sparse Core Ops, SparseCore 0:
  10.8 54.6 all-gather.2
  67.6 50.4 all-gather.4
  176.8 67.6 reduce-scatter.3
  247.8 68.0 reduce-scatter.5
  325.6 85.2 reduce-scatter.7
  415.7 117.1 all-reduce.2
where the time goes:
time: 543 us; the launch traced here: 542 us
  waiting for transfers between devices  320 us (59%)
  matrix products  121 us (22%)
  blocking collectives  41.9 us (8%)
  local copies, waits for them, and re-layouts  30.1 us (6%)
  between operations  15.5 us (3%)
  other arithmetic  12.2 us (2%)
    reduce_scatter x1, waiting for transfers between devices, on_device(): lax.psum_scatter(stacked.astype(jnp.bfloat16), 'img', scatter_dimension=1...  85.1 us
    reduce_scatter x1, waiting for transfers between devices, on_device(): lax.psum_scatter(dv_all.astype(jnp.bfloat16), 'tile', scatter_dimension=1...  68.1 us
    unnamed x7, waiting for transfers between devices  62.8 us
    all_gather x1, waiting for transfers between devices, on_device(): lax.all_gather(value_part, 'tile', axis=1, tiled=True)  47.9 us
    psum x1, blocking collectives, on_device(): grad_gain = lax.psum(jnp.sum(dh * normed, axis=0), ('img', 'tile'))  41.9 us
    all_gather x1, waiting for transfers between devices, on_device(): lax.all_gather(key_part, 'tile', axis=1, tiled=True)  40.8 us
    dot_general x1, matrix products, tile_pass(): jnp.einsum('hqk,qhd->khd', dscore, qh, preferred_element_type=jnp.float32)  34.5 us
    dot_general x1, matrix products, tile_pass(): jnp.einsum('hqk,khd->qhd', dscore, kh, preferred_element_type=jnp.float32)  30 us
  transfers between devices with their start and end apart: 6, of which 6 were waited for; matrix products, arithmetic and copies ran while one was open for 16% of the time, Pallas kernels for 0%

commit v1 on v0

v1 whole, which is shorter than its diff:
```python
import functools

import jax
import jax.numpy as jnp
import numpy as np
from jax import lax
from jax.experimental import pallas as pl
from jax.experimental.pallas import tpu as pltpu
from jax.sharding import PartitionSpec as P

HEADS = 16
TILE = 256
LANES = 128
AXES = ("img", "tile")
BF = jnp.bfloat16
F32 = jnp.float32


def nt(a, b):
    return lax.dot_general(a, b, (((1,), (1,)), ((), ())), preferred_element_type=F32)


def tn(a, b):
    return lax.dot_general(a, b, (((0,), (0,)), ((), ())), preferred_element_type=F32)


def nn(a, b):
    return jnp.dot(a, b, preferred_element_type=F32)


def attention_kernel(q_ref, d_ref, k_ref, v_ref, o_ref, dq_ref, dk_ref, dv_ref):
    width = q_ref.shape[1]
    size = width // HEADS
    scale = size ** (-0.5)

    def put(ref, first, cols, inside, value):
        value = value.astype(ref.dtype)
        if first:
            value = jnp.where(inside, value, ref[:, cols])
        ref[:, cols] = value

    for head in range(HEADS):
        low = head * size // LANES * LANES
        high = -(-(head + 1) * size // LANES) * LANES
        first = head * size - low
        cols = slice(low, high)
        lane = lax.broadcasted_iota(jnp.int32, (1, high - low), 1)
        inside = lane >= first
        mine = inside & (lane < first + size)
        q = jnp.where(mine, q_ref[:, cols], jnp.zeros((), BF))
        d = jnp.where(mine, d_ref[:, cols], jnp.zeros((), BF))
        k = k_ref[:, cols]
        v = v_ref[:, cols]
        scores = nt(q, k) * scale
        top = jnp.max(scores, axis=-1, keepdims=True)
        expo = jnp.exp(scores - top)
        probs = expo * (1.0 / jnp.sum(expo, axis=-1, keepdims=True))
        pb = probs.astype(BF)
        put(o_ref, first, cols, inside, nn(pb, v))
        dprob = nt(d, v)
        delta = jnp.sum(probs * dprob, axis=-1, keepdims=True)
        ds = (probs * (dprob - delta) * scale).astype(BF)
        put(dq_ref, first, cols, inside, nn(ds, k))
        put(dk_ref, first, cols, inside, tn(ds, q))
        put(dv_ref, first, cols, inside, tn(pb, d))


def attention(q, d, k, v):
    rows, width = q.shape
    keyrows = k.shape[0]
    vmem = pl.BlockSpec(memory_space=pltpu.VMEM)
    flops = 12 * rows * keyrows * width
    return pl.pallas_call(
        attention_kernel,
        out_shape=(
            jax.ShapeDtypeStruct((rows, width), BF),
            jax.ShapeDtypeStruct((rows, width), BF),
            jax.ShapeDtypeStruct((keyrows, width), BF),
            jax.ShapeDtypeStruct((keyrows, width), BF),
        ),
        in_specs=[vmem] * 4,
        out_specs=(vmem,) * 4,
        compiler_params=pltpu.CompilerParams(vmem_limit_bytes=40 * 2**20),
        cost_estimate=pl.CostEstimate(
            flops=4 * flops,
            bytes_accessed=2 * (4 * rows + 4 * keyrows) * width,
            transcendentals=HEADS * rows * keyrows,
        ),
        name="attention",
    )(q, d, k, v)


def on_device(n_img, n_tile, tiles, tile_image, guide, gain, w_query, w_key, w_value, w_out, grad_out):
    width = tiles.shape[1]
    images, part = guide.shape[0], guide.shape[1]
    i = lax.axis_index("img")
    t = lax.axis_index("tile")
    image = tile_image[0]
    tile_bits = [1 << b for b in range(n_tile.bit_length() - 1)]
    img_bits = [1 << b for b in range(n_img.bit_length() - 1)]

    def swap_tile(x, bit):
        return lax.ppermute(x, "tile", [(s, s ^ bit) for s in range(n_tile)])

    def swap_img(x, bit):
        return lax.ppermute(x, "img", [(s, s ^ bit) for s in range(n_img)])

    theirs = swap_tile(tile_image, 1)[0]
    blocks = guide[None]
    for bit in tile_bits[:0:-1]:
        blocks = jnp.concatenate([blocks, swap_tile(blocks, bit)], axis=0)

    def pick(arr, which):
        chosen = arr[:, 0]
        for c in range(1, images):
            chosen = jnp.where(which == c, arr[:, c], chosen)
        return chosen

    other = swap_tile(pick(blocks, theirs), 1)
    mine = pick(blocks, image)
    used = jnp.concatenate([mine, other], axis=0).reshape(-1, width)

    xf = tiles.astype(F32)
    rstd = lax.rsqrt(jnp.mean(xf * xf, axis=-1, keepdims=True) + 1e-06)
    normed = xf * rstd
    hidden = (normed * gain).astype(BF)
    query = nn(hidden, w_query).astype(BF)
    dout = nt(grad_out, w_out).astype(BF)
    keys = nn(used, w_key).astype(BF)
    values = nn(used, w_value).astype(BF)
    outv, dq, dk, dv = attention(query, dout, keys, values)

    r = width // (n_img * n_tile)
    order = np.arange(width).reshape(n_img, n_tile // 2, 2, r).transpose(2, 0, 1, 3).reshape(-1)
    onehot = (
        lax.broadcasted_iota(jnp.int32, (width, width), 0) == jnp.asarray(order, jnp.int32)[None]
    ).astype(BF)

    def reduced(left, right, tile_first):
        ordered = nn(left, onehot).astype(BF)
        x = tn(ordered, right).astype(BF)
        x = x.reshape(2, n_img // 2, 2, width // (2 * n_img), width)

        def halve(x, axis, bit, swap):
            keep = lax.dynamic_index_in_dim(x, bit, axis, keepdims=False)
            send = lax.dynamic_index_in_dim(x, 1 - bit, axis, keepdims=False)
            return (keep.astype(F32) + swap(send).astype(F32)).astype(BF)

        x = halve(x, 2, i & 1, lambda s: swap_img(s, 1))
        steps = [("img", bit) for bit in img_bits[1:]]
        steps = [("tile", 1)] + steps if tile_first else steps + [("tile", 1)]
        lead_tile = True
        for name, bit in steps:
            if name == "tile":
                x = halve(x, 0, t & 1, lambda s: swap_tile(s, 1))
                lead_tile = False
            else:
                axis = 1 if lead_tile else 0
                shape = x.shape
                x = x.reshape(shape[:axis] + (shape[axis] // 2, 2) + shape[axis + 1 :])
                x = halve(x, axis + 1, (i // bit) & 1, lambda s, bit=bit: swap_img(s, bit))
        x = x.reshape(n_tile // 2, r, width)
        for bit in tile_bits[1:]:
            x = x.reshape(x.shape[0] // 2, 2, r, width)
            x = halve(x, 1, (t // bit) & 1, lambda s, bit=bit: swap_tile(s, bit))
        return x.reshape(r, width).astype(F32)

    grad_out_w = reduced(outv, grad_out, False)
    grad_query_w = reduced(hidden, dq, True)

    term = (nt(dk, w_key) + nt(dv, w_value)).astype(BF).reshape(n_tile, part, width)
    half = n_tile // 2
    received = swap_tile(term[half:], 1).astype(F32)
    own = term[:half].astype(F32)
    x = jnp.stack(
        [jnp.where(image == c, own, 0.0) + jnp.where(theirs == c, received, 0.0) for c in range(images)],
        axis=1,
    ).astype(BF)
    for bit in tile_bits[1:]:
        half = x.shape[0] // 2
        x = (x[:half].astype(F32) + swap_tile(x[half:], bit).astype(F32)).astype(BF)
    grad_guide = x.reshape(guide.shape)

    grad_key_w = reduced(used, dk, False)
    grad_value_w = reduced(used, dv, True)

    dh = nt(dq, w_query)
    grad_gain = jnp.sum(dh * normed, axis=0)
    for bit in tile_bits:
        grad_gain = grad_gain + swap_tile(grad_gain, bit)
    for bit in img_bits:
        grad_gain = grad_gain + swap_img(grad_gain, bit)
    dn = dh * gain
    grad_tiles = (rstd * (dn - normed * jnp.mean(dn * normed, axis=-1, keepdims=True))).astype(BF)
    grad_weights = jnp.stack([grad_query_w, grad_key_w, grad_value_w, grad_out_w])
    return (grad_tiles, grad_guide, grad_weights, grad_gain)


def solution(mesh):
    return jax.shard_map(
        functools.partial(on_device, mesh.shape["img"], mesh.shape["tile"]),
        mesh=mesh,
        in_specs=(
            P(("img", "tile"), None),
            P(("img", "tile")),
            P("img", "tile", None),
            P(),
            P(),
            P(),
            P(),
            P(),
            P(("img", "tile"), None),
        ),
        out_specs=(
            P(("img", "tile"), None),
            P("img", "tile", None),
            P(None, ("img", "tile"), None),
            P(),
        ),
        check_vma=False,
    )
```

time: 543 us -> 219 us (0.40)
  waiting for transfers between devices: 320 us -> 85.8 us
  matrix products: 121 us -> 40.1 us
  blocking collectives: 41.9 us -> 0 us
  starting transfers between devices: 0.65 us -> 37.4 us
  local copies, waits for them, and re-layouts: 30.1 us -> 13.3 us
  Pallas kernels: 0 us -> 13.5 us
  between operations: 15.5 us -> 3.31 us
  other arithmetic: 12.2 us -> 21.5 us
    reduce_scatter x3 -> x0, waiting for transfers between devices: 169 us -> none  [the longest x1 85.1 us: on_device(): lax.psum_scatter(stacked.astype(jnp.bfloat16), 'img', scatter_dimension=1...]
    all_gather x2 -> x0, waiting for transfers between devices: 88.7 us -> none  [the longest x1 47.9 us: on_device(): lax.all_gather(value_part, 'tile', axis=1, tiled=True)]
    ppermute x0 -> x32, waiting for transfers between devices: none -> 85.8 us  [the longest x22 70 us: swap_tile(): return lax.ppermute(x, 'tile', [(s, s ^ bit) for s in range(n_tile)])]
    dot_general x16 -> x12, matrix products: 113 us -> 40.1 us  [the longest x4 24 us: tn(): lax.dot_general(a, b, (((0,), (0,)), ((), ())), preferred_element_type=F32)]
    unnamed x7 -> x0, waiting for transfers between devices: 62.8 us -> none
    psum x1 -> x0, blocking collectives: 41.9 us -> none  [on_device(): grad_gain = lax.psum(jnp.sum(dh * normed, axis=0), ('img', 'tile'))]
    ppermute x0 -> x32, starting transfers between devices: none -> 37.4 us  [the longest x22 32.4 us: swap_tile(): return lax.ppermute(x, 'tile', [(s, s ^ bit) for s in range(n_tile)])]
    pallas_call x0 -> x1, Pallas kernels: none -> 13.5 us  [attention(): pl.pallas_call(attention_kernel, out_shape=(jax.ShapeDtypeStruct((rows, w...]
  transfers between devices with their start and end apart: 6 -> 32, of which waited for: 6 -> 21; matrix products, arithmetic and copies ran while one was open for 16% -> 19% of each run, Pallas kernels for 0% -> 0%
where the time goes in v1:
time: 219 us; the launch traced here: 215 us
  waiting for transfers between devices  85.8 us (39%)
  matrix products  40.1 us (18%)
  starting transfers between devices  37.4 us (17%)
  other arithmetic  21.5 us (10%)
  Pallas kernels  13.5 us (6%)
  local copies, waits for them, and re-layouts  13.3 us (6%)
  between operations  3.31 us (2%)
    ppermute x22, waiting for transfers between devices, swap_tile(): return lax.ppermute(x, 'tile', [(s, s ^ bit) for s in range(n_tile)])  70 us
    ppermute x22, starting transfers between devices, swap_tile(): return lax.ppermute(x, 'tile', [(s, s ^ bit) for s in range(n_tile)])  32.4 us
    dot_general x4, matrix products, tn(): lax.dot_general(a, b, (((0,), (0,)), ((), ())), preferred_element_type=F32)  24 us
    ppermute x10, waiting for transfers between devices, swap_img(): return lax.ppermute(x, 'img', [(s, s ^ bit) for s in range(n_img)])  15.8 us
    pallas_call x1, Pallas kernels, attention(): pl.pallas_call(attention_kernel, out_shape=(jax.ShapeDtypeStruct((rows, w...  13.5 us
    squeeze x20, local copies, waits for them, and re-layouts, halve(): send = lax.dynamic_index_in_dim(x, 1 - bit, axis, keepdims=False)  10.6 us
    convert_element_type x20, other arithmetic, halve(): return (keep.astype(F32) + swap(send).astype(F32)).astype(BF)  9.97 us
    dot_general x4, matrix products, nn(): return jnp.dot(a, b, preferred_element_type=F32)  9.25 us
  transfers between devices with their start and end apart: 32, of which 21 were waited for; matrix products, arithmetic and copies ran while one was open for 19% of the time, Pallas kernels for 0%

profile of v1, /device:TPU:0, one launch (start us, length us, event | category | flops | bytes accessed | tf_op | source)
XLA Modules:
  0.0 214.8 jit_solution(7347066543452927852)
XLA Ops:
  0.7 4.1 %collective-permute-start = (bf16[1,2,64,1152]{3,2,1,0:T(8,128)(2,1)}, bf16[1,2,64,1152]{3,2,1,0:T(8,128)(2,1)S(1)}, u32[]{:S(2)}, u32[]{:S(2)}) collective-permute-start(bf16[1,2,64,1152]{3,2,1,0:T(8,128)(2,1)} %bitcast.138), channel_id=1, source_target_pairs={{0,4},{1,5},{2,6},{3,7},{4,0},{5,1},{6,2},{7,3},{8,12},{9,13},{10,... | collective-permute-start | bytes 884744 | tf_op jit(solution)/shard_map/ppermute | solution.py:103
  6.3 12.0 %collective-permute-done = bf16[1,2,64,1152]{3,2,1,0:T(8,128)(2,1)S(1)} collective-permute-done((bf16[1,2,64,1152]{3,2,1,0:T(8,128)(2,1)}, bf16[1,2,64,1152]{3,2,1,0:T(8,128)(2,1)S(1)}, u32[]{:S(2)}, u32[]{:S(2)}) %collective-permute-start) | collective-permute-done | bytes 294944 | tf_op jit(solution)/shard_map/ppermute | solution.py:103
  20.5 3.7 %convolution_convert_fusion.7.q_ref = bf16[256,1152]{1,0:T(8,128)(2,1)} fusion(bf16[1152,1152]{1,0:T(8,128)(2,1)} %param.14, bf16[256,1152]{1,0:T(8,128)(2,1)S(1)} %copy-done.16, f32[1152]{0:T(1024)S(1)} %copy-done.21, f32[256]{0:T(256)S(1)} %add_rsqrt_fusion), kind=kOutput, calls=%fused_computation.25 | convolution fusion | flops 680951808 | bytes 3839488 | tf_op jit(solution)/shard_map/dot_general | solution.py:28
  24.8 9.2 %collective-permute-done.1 = bf16[2,2,64,1152]{3,2,1,0:T(8,128)(2,1)S(1)} collective-permute-done((bf16[2,2,64,1152]{3,2,1,0:T(8,128)(2,1)S(1)}, bf16[2,2,64,1152]{3,2,1,0:T(8,128)(2,1)S(1)}, u32[]{:S(2)}, u32[]{:S(2)}) %collective-permute-start.1) | collective-permute-done | bytes 589856 | tf_op jit(solution)/shard_map/ppermute | solution.py:103
  40.4 8.9 %collective-permute-done.3 = bf16[4,64,1152]{2,1,0:T(8,128)(2,1)} collective-permute-done((bf16[4,64,1152]{2,1,0:T(8,128)(2,1)}, bf16[4,64,1152]{2,1,0:T(8,128)(2,1)}, u32[]{:S(2)}, u32[]{:S(2)}) %collective-permute-start.3) | collective-permute-done | bytes 589856 | tf_op jit(solution)/shard_map/ppermute | solution.py:103
  54.2 13.5 %attention.1 = (bf16[256,1152]{1,0:T(8,128)(2,1)S(1)}, bf16[256,1152]{1,0:T(8,128)(2,1)S(1)}, bf16[512,1152]{1,0:T(8,128)(2,1)S(1)}, bf16[512,1152]{1,0:T(8,128)(2,1)S(1)}) custom-call(bf16[256,1152]{1,0:T(8,128)(2,1)S(1)} %copy-done.2, bf16[256,1152]{1,0:T(8,128)(2,1)S(1)} %convolution_convert_fusion.6.d_ref, ...), custom_call_target="tpu_custom_call" | custom-call | flops 7247757312 | bytes 7077888 | tf_op jit(solution)/shard_map/attention/pallas_call | solution.py:73
  67.7 2.1 fusion.25
  73.6 3.2 %convolution_convert_fusion.3 = bf16[1152,1152]{1,0:T(8,128)(2,1)} fusion(bf16[512,1152]{1,0:T(8,128)(2,1)S(1)} %fusion.4, bf16[512,1152]{1,0:T(8,128)(2,1)S(1)} %get-tuple-element.9), kind=kOutput, calls=%fused_computation.3 | convolution fusion | flops 1360281600 | bytes 5013504 | tf_op jit(solution)/shard_map/dot_general | solution.py:24
  76.9 13.4 %convolution_convert_fusion.2 = bf16[1152,1152]{1,0:T(8,128)(2,1)} fusion(bf16[512,1152]{1,0:T(8,128)(2,1)S(1)} %fusion.4, bf16[512,1152]{1,0:T(8,128)(2,1)S(1)} %get-tuple-element.10), kind=kOutput, calls=%fused_computation.2 | convolution fusion | flops 1360281600 | bytes 5013504 | tf_op jit(solution)/shard_map/dot_general | solution.py:24
  95.9 3.6 %convolution_convert_fusion = bf16[1152,1152]{1,0:T(8,128)(2,1)} fusion(bf16[256,1152]{1,0:T(8,128)(2,1)S(1)} %copy-done.26, bf16[256,1152]{1,0:T(8,128)(2,1)S(1)} %copy-done.6, s32[1152]{0:T(1024)S(1)} %copy-done.27), kind=kOutput, calls=%fused_computation | convolution fusion | flops 1361903616 | bytes 3838464 | tf_op jit(solution)/shard_map/dot_general | solution.py:24
  99.5 2.6 %dynamic-slice_bitcast_fusion = bf16[2,2,144,1152]{3,2,1,0:T(8,128)(2,1)} fusion(bf16[2,2,2,144,1152]{4,3,2,1,0:T(8,128)(2,1)} %bitcast.134, s32[]{:T(128)S(6)} %select_n.156), kind=kLoop, calls=%fused_computation.43 | loop fusion | bytes 2654212 | tf_op jit(solution)/shard_map/jit(dynamic_index_in_dim)/squeeze | solution.py:146
  104.3 3.3 %collective-permute-done.27 = f32[1152]{0:T(1024)S(1)} collective-permute-done((f32[1152]{0:T(1024)S(1)}, f32[1152]{0:T(1024)S(1)}, u32[]{:S(2)}, u32[]{:S(2)}) %collective-permute-start.27) | collective-permute-done | bytes 4640 | tf_op jit(solution)/shard_map/ppermute | solution.py:103
  107.6 3.2 %collective-permute-start.28 = (f32[1152]{0:T(1024)S(1)}, f32[1152]{0:T(1024)S(1)}, u32[]{:S(2)}, u32[]{:S(2)}) collective-permute-start(f32[1152]{0:T(1024)S(1)} %add.213), channel_id=1, source_target_pairs={{0,2},{1,3},{2,0},{3,1},{4,6},{5,7},{6,4},{7,5},{8,10},{9,11},{10,... | collective-permute-start | bytes 13832 | tf_op jit(solution)/shard_map/ppermute | solution.py:103
  112.4 4.2 %collective-permute-start.29 = (f32[1152]{0:T(1024)S(1)}, f32[1152]{0:T(1024)S(1)}, u32[]{:S(2)}, u32[]{:S(2)}) collective-permute-start(f32[1152]{0:T(1024)S(1)} %add.214), channel_id=1, source_target_pairs={{0,4},{1,5},{2,6},{3,7},{4,0},{5,1},{6,2},{7,3},{8,12},{9,13},{10,... | collective-permute-start | bytes 13832 | tf_op jit(solution)/shard_map/ppermute | solution.py:103
  120.9 3.7 %convolution_convert_fusion.1 = bf16[1152,1152]{1,0:T(8,128)(2,1)} fusion(bf16[256,1152]{1,0:T(8,128)(2,1)S(1)} %copy-done.4, s32[1152]{0:T(1024)S(1)} %copy-done.27, bf16[256,1152]{1,0:T(8,128)(2,1)S(1)} %copy-done.18, f32[1152]{0:T(1024)S(1)} %copy-done.21, f32[256]{0:T(256)S(1)} %add_rsqrt_fusion), kind=kOutput, calls=%fused_computation.1 | convolution fusion | flops 1363083264 | bytes 3844096 | tf_op jit(solution)/shard_map/dot_general | solution.py:24
  128.9 6.8 %collective-permute-done.5 = bf16[2,2,64,1152]{3,2,1,0:T(8,128)(2,1)} collective-permute-done((bf16[2,2,64,1152]{3,2,1,0:T(8,128)(2,1)S(1)}, bf16[2,2,64,1152]{3,2,1,0:T(8,128)(2,1)}, u32[]{:S(2)}, u32[]{:S(2)}) %collective-permute-start.5) | collective-permute-done | bytes 589856 | tf_op jit(solution)/shard_map/ppermute | solution.py:103
  136.9 3.0 %collective-permute-start.6 = (bf16[1,2,64,1152]{3,2,1,0:T(8,128)(2,1)S(1)}, bf16[1,2,64,1152]{3,2,1,0:T(8,128)(2,1)S(1)}, u32[]{:S(2)}, u32[]{:S(2)}) collective-permute-start(bf16[1,2,64,1152]{3,2,1,0:T(8,128)(2,1)S(1)} %slice.46), channel_id=1, source_target_pairs={{0,4},{1,5},{2,6},{3,7},{4,0},{5,1},{6,2},{7,3},{8,12},{9,13},{10,... | collective-permute-start | bytes 884744 | tf_op jit(solution)/shard_map/ppermute | solution.py:103
  150.2 2.9 %collective-permute-done.6 = bf16[1,2,64,1152]{3,2,1,0:T(8,128)(2,1)S(1)} collective-permute-done((bf16[1,2,64,1152]{3,2,1,0:T(8,128)(2,1)S(1)}, bf16[1,2,64,1152]{3,2,1,0:T(8,128)(2,1)S(1)}, u32[]{:S(2)}, u32[]{:S(2)}) %collective-permute-start.6) | collective-permute-done | bytes 294944 | tf_op jit(solution)/shard_map/ppermute | solution.py:103
  153.8 5.8 %collective-permute-done.23 = bf16[2,1,144,1152]{3,2,1,0:T(8,128)(2,1)S(1)} collective-permute-done((bf16[2,1,144,1152]{3,2,1,0:T(8,128)(2,1)S(1)}, bf16[2,1,144,1152]{3,2,1,0:T(8,128)(2,1)S(1)}, u32[]{:S(2)}, u32[]{:S(2)}) %collective-permute-start.23) | collective-permute-done | bytes 663584 | tf_op jit(solution)/shard_map/ppermute | solution.py:106
  164.6 9.3 %collective-permute-done.13 = bf16[2,1,144,1152]{3,2,1,0:T(8,128)(2,1)S(1)} collective-permute-done((bf16[2,1,144,1152]{3,2,1,0:T(8,128)(2,1)S(1)}, bf16[2,1,144,1152]{3,2,1,0:T(8,128)(2,1)S(1)}, u32[]{:S(2)}, u32[]{:S(2)}) %collective-permute-start.13) | collective-permute-done | bytes 663584 | tf_op jit(solution)/shard_map/ppermute | solution.py:106
  178.8 5.6 %collective-permute-done.24 = bf16[1,144,1152]{2,1,0:T(8,128)(2,1)S(1)} collective-permute-done((bf16[1,144,1152]{2,1,0:T(8,128)(2,1)S(1)}, bf16[1,144,1152]{2,1,0:T(8,128)(2,1)S(1)}, u32[]{:S(2)}, u32[]{:S(2)}) %collective-permute-start.24) | collective-permute-done | bytes 331808 | tf_op jit(solution)/shard_map/ppermute | solution.py:103
  194.8 3.1 %collective-permute-done.20 = bf16[2,36,1152]{2,1,0:T(8,128)(2,1)S(1)} collective-permute-done((bf16[2,36,1152]{2,1,0:T(8,128)(2,1)}, bf16[2,36,1152]{2,1,0:T(8,128)(2,1)S(1)}, u32[]{:S(2)}, u32[]{:S(2)}) %collective-permute-start.20) | collective-permute-done | bytes 165920 | tf_op jit(solution)/shard_map/ppermute | solution.py:103
  198.1 5.5 %collective-permute-done.15 = bf16[2,36,1152]{2,1,0:T(8,128)(2,1)S(1)} collective-permute-done((bf16[2,36,1152]{2,1,0:T(8,128)(2,1)S(1)}, bf16[2,36,1152]{2,1,0:T(8,128)(2,1)S(1)}, u32[]{:S(2)}, u32[]{:S(2)}) %collective-permute-start.15) | collective-permute-done | bytes 165920 | tf_op jit(solution)/shard_map/ppermute | solution.py:103
  206.8 4.2 %collective-permute-done.21 = bf16[1,36,1152]{2,1,0:T(8,128)(2,1)S(1)} collective-permute-done((bf16[1,36,1152]{2,1,0:T(8,128)(2,1)S(1)}, bf16[1,36,1152]{2,1,0:T(8,128)(2,1)S(1)}, u32[]{:S(2)}, u32[]{:S(2)}) %collective-permute-start.21) | collective-permute-done | bytes 82976 | tf_op jit(solution)/shard_map/ppermute | solution.py:103
  (176 shorter events, 74.5 us)
Async XLA Ops:
  0.7 17.6 %collective-permute-start = (bf16[1,2,64,1152]{3,2,1,0:T(8,128)(2,1)}, bf16[1,2,64,1152]{3,2,1,0:T(8,128)(2,1)S(1)}, u32[]{:S(2)}, u32[]{:S(2)}) collective-permute-start(bf16[1,2,64,1152]{3,2,1,0:T(8,128)(2,1)} %bitcast.138), channel_id=1, source_target_pairs={{0,4},{1,5},{2,6},{3,7},{4,0},{5,1},{6,2},{7,3},{8,12},{9,13},{10,... | collective-permute-start | bytes 884744 | tf_op jit(solution)/shard_map/ppermute | solution.py:103
  4.8 19.4 %collective-permute-start.2 = (s32[1]{0:T(128)}, s32[1]{0:T(128)}, u32[]{:S(2)}, u32[]{:S(2)}) collective-permute-start(s32[1]{0:T(128)} %param.11), channel_id=1, source_target_pairs={{0,1},{1,0},{2,3},{3,2},{4,5},{5,4},{6,7},{7,6},{8,9},{9,8},{10,11... | collective-permute-start | bytes 20 | tf_op jit(solution)/shard_map/ppermute | solution.py:103
  19.3 14.6 %collective-permute-start.1 = (bf16[2,2,64,1152]{3,2,1,0:T(8,128)(2,1)S(1)}, bf16[2,2,64,1152]{3,2,1,0:T(8,128)(2,1)S(1)}, u32[]{:S(2)}, u32[]{:S(2)}) collective-permute-start(bf16[2,2,64,1152]{3,2,1,0:T(8,128)(2,1)S(1)} %pad_maximum_fusion.3), channel_id=1, source_target_pairs={{0,2},{1,3},{2,0},{3,1},{4,6},{5,7},{6,4},{7,5},{8,10},{9,11},{10,... | collective-permute-start | bytes 1769480 | tf_op jit(solution)/shard_map/ppermute | solution.py:103
  35.3 13.9 %collective-permute-start.3 = (bf16[4,64,1152]{2,1,0:T(8,128)(2,1)}, bf16[4,64,1152]{2,1,0:T(8,128)(2,1)}, u32[]{:S(2)}, u32[]{:S(2)}) collective-permute-start(bf16[4,64,1152]{2,1,0:T(8,128)(2,1)} %select_bitcast_fusion), channel_id=1, source_target_pairs={{0,1},{1,0},{2,3},{3,2},{4,5},{5,4},{6,7},{7,6},{8,9},{9,8},{10,11... | collective-permute-start | bytes 1769480 | tf_op jit(solution)/shard_map/ppermute | solution.py:103
  94.5 23.7 %collective-permute-start.4 = (bf16[4,64,1152]{2,1,0:T(8,128)(2,1)}, bf16[4,64,1152]{2,1,0:T(8,128)(2,1)}, u32[]{:S(2)}, u32[]{:S(2)}) collective-permute-start(bf16[4,64,1152]{2,1,0:T(8,128)(2,1)} %bitcast.11), channel_id=1, source_target_pairs={{0,1},{1,0},{2,3},{3,2},{4,5},{5,4},{6,7},{7,6},{8,9},{9,8},{10,11... | collective-permute-start | bytes 1769480 | tf_op jit(solution)/shard_map/ppermute | solution.py:103
  102.2 37.7 %collective-permute-start.22 = (bf16[2,2,144,1152]{3,2,1,0:T(8,128)(2,1)}, bf16[2,2,144,1152]{3,2,1,0:T(8,128)(2,1)}, u32[]{:S(2)}, u32[]{:S(2)}) collective-permute-start(bf16[2,2,144,1152]{3,2,1,0:T(8,128)(2,1)} %dynamic-slice_bitcast_fusion), channel_id=1, source_target_pairs={{0,8},{8,0},{16,24},{24,16},{1,9},{9,1},{17,25},{25,17},{2,10},{10... | collective-permute-start | bytes 3981320 | tf_op jit(solution)/shard_map/ppermute | solution.py:106
  104.0 39.3 %collective-permute-start.17 = (bf16[2,2,144,1152]{3,2,1,0:T(8,128)(2,1)}, bf16[2,2,144,1152]{3,2,1,0:T(8,128)(2,1)}, u32[]{:S(2)}, u32[]{:S(2)}) collective-permute-start(bf16[2,2,144,1152]{3,2,1,0:T(8,128)(2,1)} %dynamic-slice_bitcast_fusion.1), channel_id=1, source_target_pairs={{0,8},{8,0},{16,24},{24,16},{1,9},{9,1},{17,25},{25,17},{2,10},{10... | collective-permute-start | bytes 3981320 | tf_op jit(solution)/shard_map/ppermute | solution.py:106
  112.0 34.7 %collective-permute-start.12 = (bf16[2,2,144,1152]{3,2,1,0:T(8,128)(2,1)}, bf16[2,2,144,1152]{3,2,1,0:T(8,128)(2,1)}, u32[]{:S(2)}, u32[]{:S(2)}) collective-permute-start(bf16[2,2,144,1152]{3,2,1,0:T(8,128)(2,1)} %dynamic-slice_bitcast_fusion.2), channel_id=1, source_target_pairs={{0,8},{8,0},{16,24},{24,16},{1,9},{9,1},{17,25},{25,17},{2,10},{10... | collective-permute-start | bytes 3981320 | tf_op jit(solution)/shard_map/ppermute | solution.py:106
  119.7 15.9 %collective-permute-start.5 = (bf16[2,2,64,1152]{3,2,1,0:T(8,128)(2,1)S(1)}, bf16[2,2,64,1152]{3,2,1,0:T(8,128)(2,1)}, u32[]{:S(2)}, u32[]{:S(2)}) collective-permute-start(bf16[2,2,64,1152]{3,2,1,0:T(8,128)(2,1)S(1)} %pad_maximum_fusion.2), channel_id=1, source_target_pairs={{0,2},{1,3},{2,0},{3,1},{4,6},{5,7},{6,4},{7,5},{8,10},{9,11},{10,... | collective-permute-start | bytes 1769480 | tf_op jit(solution)/shard_map/ppermute | solution.py:103
  128.3 20.9 %collective-permute-start.7 = (bf16[2,2,144,1152]{3,2,1,0:T(8,128)(2,1)S(1)}, bf16[2,2,144,1152]{3,2,1,0:T(8,128)(2,1)S(1)}, u32[]{:S(2)}, u32[]{:S(2)}) collective-permute-start(bf16[2,2,144,1152]{3,2,1,0:T(8,128)(2,1)S(1)} %dynamic-slice_bitcast_fusion.3), channel_id=1, source_target_pairs={{0,8},{8,0},{16,24},{24,16},{1,9},{9,1},{17,25},{25,17},{2,10},{10... | collective-permute-start | bytes 3981320 | tf_op jit(solution)/shard_map/ppermute | solution.py:106
  136.9 16.2 %collective-permute-start.6 = (bf16[1,2,64,1152]{3,2,1,0:T(8,128)(2,1)S(1)}, bf16[1,2,64,1152]{3,2,1,0:T(8,128)(2,1)S(1)}, u32[]{:S(2)}, u32[]{:S(2)}) collective-permute-start(bf16[1,2,64,1152]{3,2,1,0:T(8,128)(2,1)S(1)} %slice.46), channel_id=1, source_target_pairs={{0,4},{1,5},{2,6},{3,7},{4,0},{5,1},{6,2},{7,3},{8,12},{9,13},{10,... | collective-permute-start | bytes 884744 | tf_op jit(solution)/shard_map/ppermute | solution.py:103
  141.7 17.9 %collective-permute-start.23 = (bf16[2,1,144,1152]{3,2,1,0:T(8,128)(2,1)S(1)}, bf16[2,1,144,1152]{3,2,1,0:T(8,128)(2,1)S(1)}, u32[]{:S(2)}, u32[]{:S(2)}) collective-permute-start(bf16[2,1,144,1152]{3,2,1,0:T(8,128)(2,1)S(1)} %constant_dynamic-slice_fusion.1), channel_id=1, source_target_pairs={{0,16},{8,24},{16,0},{24,8},{1,17},{9,25},{17,1},{25,9},{2,18},{10... | collective-permute-start | bytes 1990664 | tf_op jit(solution)/shard_map/ppermute | solution.py:106
  145.2 17.9 %collective-permute-start.18 = (bf16[2,144,1152]{2,1,0:T(8,128)(2,1)S(1)}, bf16[2,144,1152]{2,1,0:T(8,128)(2,1)S(1)}, u32[]{:S(2)}, u32[]{:S(2)}) collective-permute-start(bf16[2,144,1152]{2,1,0:T(8,128)(2,1)S(1)} %dynamic-slice_bitcast_fusion.4), channel_id=1, source_target_pairs={{0,1},{1,0},{2,3},{3,2},{4,5},{5,4},{6,7},{7,6},{8,9},{9,8},{10,11... | collective-permute-start | bytes 1990664 | tf_op jit(solution)/shard_map/ppermute | solution.py:103
  148.6 25.3 %collective-permute-start.13 = (bf16[2,1,144,1152]{3,2,1,0:T(8,128)(2,1)S(1)}, bf16[2,1,144,1152]{3,2,1,0:T(8,128)(2,1)S(1)}, u32[]{:S(2)}, u32[]{:S(2)}) collective-permute-start(bf16[2,1,144,1152]{3,2,1,0:T(8,128)(2,1)S(1)} %constant_dynamic-slice_fusion.5), channel_id=1, source_target_pairs={{0,16},{8,24},{16,0},{24,8},{1,17},{9,25},{17,1},{25,9},{2,18},{10... | collective-permute-start | bytes 1990664 | tf_op jit(solution)/shard_map/ppermute | solution.py:106
  149.6 27.7 %collective-permute-start.8 = (bf16[2,144,1152]{2,1,0:T(8,128)(2,1)S(1)}, bf16[2,144,1152]{2,1,0:T(8,128)(2,1)S(1)}, u32[]{:S(2)}, u32[]{:S(2)}) collective-permute-start(bf16[2,144,1152]{2,1,0:T(8,128)(2,1)S(1)} %dynamic-slice_bitcast_fusion.5), channel_id=1, source_target_pairs={{0,1},{1,0},{2,3},{3,2},{4,5},{5,4},{6,7},{7,6},{8,9},{9,8},{10,11... | collective-permute-start | bytes 1990664 | tf_op jit(solution)/shard_map/ppermute | solution.py:103
  159.9 24.5 %collective-permute-start.24 = (bf16[1,144,1152]{2,1,0:T(8,128)(2,1)S(1)}, bf16[1,144,1152]{2,1,0:T(8,128)(2,1)S(1)}, u32[]{:S(2)}, u32[]{:S(2)}) collective-permute-start(bf16[1,144,1152]{2,1,0:T(8,128)(2,1)S(1)} %dynamic-slice_bitcast_fusion.6), channel_id=1, source_target_pairs={{0,1},{1,0},{2,3},{3,2},{4,5},{5,4},{6,7},{7,6},{8,9},{9,8},{10,11... | collective-permute-start | bytes 995336 | tf_op jit(solution)/shard_map/ppermute | solution.py:103
  164.0 22.4 %collective-permute-start.19 = (bf16[1,144,1152]{2,1,0:T(8,128)(2,1)}, bf16[1,144,1152]{2,1,0:T(8,128)(2,1)}, u32[]{:S(2)}, u32[]{:S(2)}) collective-permute-start(bf16[1,144,1152]{2,1,0:T(8,128)(2,1)} %constant_dynamic-slice_fusion.3), channel_id=1, source_target_pairs={{0,16},{8,24},{16,0},{24,8},{1,17},{9,25},{17,1},{25,9},{2,18},{10... | collective-permute-start | bytes 995336 | tf_op jit(solution)/shard_map/ppermute | solution.py:106
  174.8 15.0 %collective-permute-start.14 = (bf16[1,144,1152]{2,1,0:T(8,128)(2,1)}, bf16[1,144,1152]{2,1,0:T(8,128)(2,1)}, u32[]{:S(2)}, u32[]{:S(2)}) collective-permute-start(bf16[1,144,1152]{2,1,0:T(8,128)(2,1)} %dynamic-slice_bitcast_fusion.7), channel_id=1, source_target_pairs={{0,1},{1,0},{2,3},{3,2},{4,5},{5,4},{6,7},{7,6},{8,9},{9,8},{10,11... | collective-permute-start | bytes 995336 | tf_op jit(solution)/shard_map/ppermute | solution.py:103
  178.3 13.9 %collective-permute-start.9 = (bf16[1,144,1152]{2,1,0:T(8,128)(2,1)}, bf16[1,144,1152]{2,1,0:T(8,128)(2,1)}, u32[]{:S(2)}, u32[]{:S(2)}) collective-permute-start(bf16[1,144,1152]{2,1,0:T(8,128)(2,1)} %constant_dynamic-slice_fusion.7), channel_id=1, source_target_pairs={{0,16},{8,24},{16,0},{24,8},{1,17},{9,25},{17,1},{25,9},{2,18},{10... | collective-permute-start | bytes 995336 | tf_op jit(solution)/shard_map/ppermute | solution.py:106
  188.2 9.7 %collective-permute-start.20 = (bf16[2,36,1152]{2,1,0:T(8,128)(2,1)}, bf16[2,36,1152]{2,1,0:T(8,128)(2,1)S(1)}, u32[]{:S(2)}, u32[]{:S(2)}) collective-permute-start(bf16[2,36,1152]{2,1,0:T(8,128)(2,1)} %dynamic-slice_bitcast_fusion.9), channel_id=1, source_target_pairs={{0,2},{1,3},{2,0},{3,1},{4,6},{5,7},{6,4},{7,5},{8,10},{9,11},{10,... | collective-permute-start | bytes 497672 | tf_op jit(solution)/shard_map/ppermute | solution.py:103
  191.0 12.6 %collective-permute-start.15 = (bf16[2,36,1152]{2,1,0:T(8,128)(2,1)S(1)}, bf16[2,36,1152]{2,1,0:T(8,128)(2,1)S(1)}, u32[]{:S(2)}, u32[]{:S(2)}) collective-permute-start(bf16[2,36,1152]{2,1,0:T(8,128)(2,1)S(1)} %dynamic-slice_bitcast_fusion.10), channel_id=1, source_target_pairs={{0,2},{1,3},{2,0},{3,1},{4,6},{5,7},{6,4},{7,5},{8,10},{9,11},{10,... | collective-permute-start | bytes 497672 | tf_op jit(solution)/shard_map/ppermute | solution.py:103
  193.3 12.2 %collective-permute-start.10 = (bf16[2,36,1152]{2,1,0:T(8,128)(2,1)S(1)}, bf16[2,36,1152]{2,1,0:T(8,128)(2,1)S(1)}, u32[]{:S(2)}, u32[]{:S(2)}) collective-permute-start(bf16[2,36,1152]{2,1,0:T(8,128)(2,1)S(1)} %dynamic-slice_bitcast_fusion.11), channel_id=1, source_target_pairs={{0,2},{1,3},{2,0},{3,1},{4,6},{5,7},{6,4},{7,5},{8,10},{9,11},{10,... | collective-permute-start | bytes 497672 | tf_op jit(solution)/shard_map/ppermute | solution.py:103
  194.4 12.4 %collective-permute-start.26 = (bf16[1,36,1152]{2,1,0:T(8,128)(2,1)S(1)}, bf16[1,36,1152]{2,1,0:T(8,128)(2,1)S(1)}, u32[]{:S(2)}, u32[]{:S(2)}) collective-permute-start(bf16[1,36,1152]{2,1,0:T(8,128)(2,1)S(1)} %constant_dynamic-slice_fusion), channel_id=1, source_target_pairs={{0,4},{1,5},{2,6},{3,7},{4,0},{5,1},{6,2},{7,3},{8,12},{9,13},{10,... | collective-permute-start | bytes 248840 | tf_op jit(solution)/shard_map/ppermute | solution.py:103
  198.0 13.0 %collective-permute-start.21 = (bf16[1,36,1152]{2,1,0:T(8,128)(2,1)S(1)}, bf16[1,36,1152]{2,1,0:T(8,128)(2,1)S(1)}, u32[]{:S(2)}, u32[]{:S(2)}) collective-permute-start(bf16[1,36,1152]{2,1,0:T(8,128)(2,1)S(1)} %constant_dynamic-slice_fusion.2), channel_id=1, source_target_pairs={{0,4},{1,5},{2,6},{3,7},{4,0},{5,1},{6,2},{7,3},{8,12},{9,13},{10,... | collective-permute-start | bytes 248840 | tf_op jit(solution)/shard_map/ppermute | solution.py:103
  (36 other events, 262.8 us)
